TPU v7x, 32 devices: a whole 2x2x4 slice. The times are simulated.
32 devices in a mesh: seq: 8 (over y, x, core), tensor: 4 (over z).
Axes of the slice: x: 2, y: 2, z: 4, core: 2. Of those that a mesh axis runs over, the one named last changes fastest.
Arguments:
- tokens: bfloat16 [6144, 2048], P('seq'), may hold values from -6 to 6
- norm_gain: float32 [2048], replicated, may hold values from 0.1 to 1.9
- query_weight: bfloat16 [2048, 2048], P(None, 'tensor'), may hold values from -0.125 to 0.125
- key_value_matrix: bfloat16 [2048, 4, 128], replicated, may hold values from -0.125 to 0.125
- out_weight: bfloat16 [2048, 2048], replicated, may hold values from -0.125 to 0.125
- cache_pages: bfloat16 [512, 4, 128, 128], P('seq'), may hold values from -180 to 180, as said below
- page_table: int32 [8, 64], replicated, may hold values from 0 to 511, as said below
- request_lengths: int32 [40], replicated, may hold values from 1 to 764, as said below
- request_groups: int32 [40], replicated, may hold values from 0 to 7
Outputs:
- projected: bfloat16 [6144, 2048], P('seq', 'tensor')
Inputs may be any that keep to these rules, and one draw needn't show every extreme that they name: `page_table`: every page id appears once. Of the last 16 entries of each row, exactly 2 lie in each block of 64 consecutive ids, the pages held by one seq device. `request_lengths`: the lengths of the 5 requests of one seq device sum to at most 768, and to exactly 768 on at least one device. `cache_pages`: keys in the first 64 entries of the last dimension, values in the rest.
All inputs are finite; a program needn't handle non-finite values.
Results may differ from a plain program's by a relative error of at most 0.012.
The roundings to bfloat16 on the way count: a program that leaves them out, or rounds other values in their place, can miss the bound.
Values may be sent and summed in bfloat16 or wider, within the bound.
A program may use at most 128 MiB of HBM per device.

v0:
```python
import math

import jax
import jax.numpy as jnp
from jax import lax
from jax.sharding import PartitionSpec as P

QUERY_HEADS = 32
KEY_VALUE_HEADS = 4
HEAD_SIZE = 64
WINDOW_LENGTH = 2048
DEVICE_REQUESTS = 5
PPG = 64
WP = 16


MASKED_SCORE = -1e30


def normalize(tokens, norm_gain):
    widened = tokens.astype(jnp.float32)
    factor = lax.rsqrt(jnp.mean(widened * widened, axis=-1, keepdims=True) + 1e-05)
    return (widened * factor * norm_gain).astype(jnp.bfloat16)


def row_layout(lengths, row_total_count):
    request_ends = jnp.cumsum(lengths)
    starts = request_ends - lengths
    slot_ids = lax.iota(jnp.int32, row_total_count)
    row_request = jnp.sum((slot_ids[:, None] >= request_ends[None, :]).astype(jnp.int32), axis=1)
    row_live = slot_ids < request_ends[-1]
    choose = row_request[:, None] == lax.iota(jnp.int32, lengths.shape[0])[None, :]
    begins = jnp.sum(jnp.where(choose, starts[None, :], 0), axis=1)
    return (row_request, row_live, slot_ids - begins)


def lookup_rows(table, wanted):
    table_rows = table.shape[0]
    matches = wanted[:, None] == lax.iota(jnp.int32, table_rows)[None, :]
    return jnp.sum(jnp.where(matches[:, :, None], table[None, :, :], 0), axis=1)


def body(
    tokens,
    norm_gain,
    query_weight,
    key_value_matrix,
    out_weight,
    cache_pages,
    page_table,
    request_lengths,
    request_groups,
):
    seq_count = lax.axis_size("seq")
    seq_index = lax.axis_index("seq")
    tensor_rank_index = lax.axis_index("tensor")
    row_count = tokens.shape[0]
    resident_heads = query_weight.shape[1] // HEAD_SIZE
    key_value_head = tensor_rank_index * resident_heads // (QUERY_HEADS // KEY_VALUE_HEADS)
    group_count = page_table.shape[0]
    per_owner = WP // seq_count
    pages_here = cache_pages.shape[0]
    score_scale = HEAD_SIZE ** (-0.5)
    normed = normalize(tokens, norm_gain)
    query_rows = jnp.dot(normed, query_weight, preferred_element_type=jnp.float32).astype(
        jnp.bfloat16
    )
    query_rows = query_rows.reshape(row_count, resident_heads, HEAD_SIZE)
    head_weight = lax.dynamic_index_in_dim(key_value_matrix, key_value_head, 1, keepdims=False)
    new_token_rows = jnp.dot(normed, head_weight, preferred_element_type=jnp.float32).astype(
        jnp.bfloat16
    )
    lengths = lax.dynamic_slice_in_dim(
        request_lengths, seq_index * DEVICE_REQUESTS, DEVICE_REQUESTS
    )
    my_groups = lax.dynamic_slice_in_dim(
        request_groups, seq_index * DEVICE_REQUESTS, DEVICE_REQUESTS
    )
    row_request, row_live, row_position = row_layout(lengths, row_count)
    tail_ids = page_table[:, PPG - WP :]
    holder = tail_ids // pages_here
    local_slot = tail_ids % pages_here
    earlier = lax.iota(jnp.int32, WP)[:, None] > lax.iota(jnp.int32, WP)[None, :]
    same_owner = holder[:, :, None] == holder[:, None, :]
    tail_rank = jnp.sum((same_owner & earlier[None, :, :]).astype(jnp.int32), axis=2)
    tail_hit = (holder == seq_index)[:, :, None] & (
        tail_rank[:, :, None] == lax.iota(jnp.int32, per_owner)[None, None, :]
    )
    tail_pick = jnp.sum(jnp.where(tail_hit, local_slot[:, :, None], 0), axis=1)
    head_pages = lax.dynamic_index_in_dim(cache_pages, key_value_head, 1, keepdims=False)
    my_holder = lookup_rows(holder, my_groups)
    my_rank = lookup_rows(tail_rank, my_groups)
    outgoing = head_pages[tail_pick.reshape(-1)]
    gathered = lax.all_gather(outgoing, "seq", axis=0, tiled=True)
    where_from = my_holder * (group_count * per_owner) + my_groups[:, None] * per_owner + my_rank
    window_rows = gathered[where_from.reshape(-1)]
    window_rows = window_rows.reshape(DEVICE_REQUESTS, WINDOW_LENGTH, 2 * HEAD_SIZE)
    offsets = lax.iota(jnp.int32, WINDOW_LENGTH)
    column = lax.iota(jnp.int32, row_count)
    fresh_keys = new_token_rows[:, :HEAD_SIZE]
    fresh_values = new_token_rows[:, HEAD_SIZE:]
    block_size = math.gcd(row_count, 128)
    block_count = row_count // block_size

    def one_block(block_inputs):
        block_query, block_request, block_live, block_position, block_column = block_inputs
        first_request = jnp.min(block_request)
        last_request = jnp.minimum(jnp.max(block_request), DEVICE_REQUESTS - 1)

        def add_scores(request_slot, running):
            keys_here = lax.dynamic_index_in_dim(window_rows, request_slot, 0, keepdims=False)[
                :, :HEAD_SIZE
            ]
            scores_one = (
                jnp.einsum(
                    "rhd,md->hrm", block_query, keys_here, preferred_element_type=jnp.float32
                )
                * score_scale
            )
            return jnp.where((block_request == request_slot)[None, :, None], scores_one, running)

        prefix_scores = lax.fori_loop(
            first_request,
            last_request + 1,
            add_scores,
            jnp.zeros((resident_heads, block_size, WINDOW_LENGTH), jnp.float32),
        )
        suffix_scores = (
            jnp.einsum("rhd,cd->hrc", block_query, fresh_keys, preferred_element_type=jnp.float32)
            * score_scale
        )
        prefix_mask = block_live[:, None] & (offsets[None, :] >= block_position[:, None] + 1)
        suffix_mask = (
            (block_request[:, None] == row_request[None, :])
            & block_live[:, None]
            & (column[None, :] <= block_column[:, None])
            & (block_column[:, None] - column[None, :] < WINDOW_LENGTH)
        )
        row_top = jnp.maximum(
            jnp.max(jnp.where(prefix_mask[None], prefix_scores, MASKED_SCORE), axis=2),
            jnp.max(jnp.where(suffix_mask[None], suffix_scores, MASKED_SCORE), axis=2),
        )
        prefix_raw = jnp.where(prefix_mask[None], jnp.exp(prefix_scores - row_top[:, :, None]), 0.0)
        suffix_raw = jnp.where(suffix_mask[None], jnp.exp(suffix_scores - row_top[:, :, None]), 0.0)
        row_total = jnp.sum(prefix_raw, axis=2) + jnp.sum(suffix_raw, axis=2)
        prefix_weights = prefix_raw.astype(jnp.bfloat16)
        suffix_weights = suffix_raw.astype(jnp.bfloat16)
        weighted = jnp.einsum(
            "hrc,cd->rhd", suffix_weights, fresh_values, preferred_element_type=jnp.float32
        )

        def add_values(request_slot, running):
            values_here = lax.dynamic_index_in_dim(window_rows, request_slot, 0, keepdims=False)[
                :, HEAD_SIZE:
            ]
            chosen = jnp.where(
                (block_request == request_slot)[None, :, None],
                prefix_weights,
                jnp.zeros((), jnp.bfloat16),
            )
            return running + jnp.einsum(
                "hrm,md->rhd", chosen, values_here, preferred_element_type=jnp.float32
            )

        weighted = lax.fori_loop(first_request, last_request + 1, add_values, weighted)
        safe_total = jnp.where(block_live[None, :], row_total, 1.0)
        block_out = jnp.where(
            block_live[:, None, None], weighted / jnp.transpose(safe_total)[:, :, None], 0.0
        )
        return block_out.astype(jnp.bfloat16).reshape(block_size, resident_heads * HEAD_SIZE)

    block_inputs = (
        query_rows.reshape(block_count, block_size, resident_heads, HEAD_SIZE),
        row_request.reshape(block_count, block_size),
        row_live.reshape(block_count, block_size),
        row_position.reshape(block_count, block_size),
        column.reshape(block_count, block_size),
    )
    attended = lax.map(one_block, block_inputs).reshape(row_count, resident_heads * HEAD_SIZE)
    my_rows = lax.dynamic_slice_in_dim(
        out_weight, tensor_rank_index * resident_heads * HEAD_SIZE, resident_heads * HEAD_SIZE, 0
    )
    partial_terms = jnp.dot(attended, my_rows, preferred_element_type=jnp.float32)
    projected = lax.psum_scatter(partial_terms, "tensor", scatter_dimension=1, tiled=True)
    return projected.astype(jnp.bfloat16)


def solution(mesh):
    return jax.shard_map(
        body,
        mesh=mesh,
        in_specs=(
            P("seq", None),
            P(),
            P(None, "tensor"),
            P(),
            P(),
            P("seq", None, None, None),
            P(),
            P(),
            P(),
        ),
        out_specs=P("seq", "tensor"),
        check_vma=False,
    )
```

profile of v0, /device:TPU:0, one launch (start us, length us, event | category | flops | bytes accessed | tf_op | source)
XLA Modules:
  0.0 534.7 jit_solution(4888461040493703357)
XLA Ops:
  8.9 3.2 dynamic-slice_bitcast_fusion.4
  12.1 3.0 gather_fusion
  16.4 2.8 fusion.43
  24.0 2.4 constant_dynamic-slice_fusion.3
  26.4 3.2 convolution_convert_fusion.1
  29.6 25.1 %all-gather.3.cloned.1.call-done = bf16[128,128,128]{2,1,0:T(8,128)(2,1)} async-done(((bf16[16,128,128]{2,1,0:T(8,128)(2,1)}), bf16[128,128,128]{2,1,0:T(8,128)(2,1)}) %all-gather.3.cloned.1.call-update) | async-done | bytes 4194320 | tf_op jit(solution)/shard_map/all_gather | solution.py:94
  54.7 4.8 gather_fusion.1
  59.5 4.6 copy.37
  64.0 326.3 %while.38 = (s32[]{:T(128)}, bf16[6,128,512]{2,1,0:T(8,128)(2,1)S(1)}, pred[6,128]{1,0:T(8,128)(4,1)S(1)}, s32[6,128]{1,0:T(8,128)S(1)}, s32[768]{0:T(1024)S(1)}...) while((s32[]{:T(128)}, ...), condition=%wide.region_19.20_spmd.clone.clone, body=%wide.region_8.19_spmd.clone.clone.sunk | while | flops 767196800 | bytes 116395192 | solution.py:179
  66.1 3.9 broadcast.253.clone.2
  70.0 18.0 %while.39 = (s32[]{:T(128)}, f32[8,128,2048]{1,2,0:T(8,128)}, s32[]{:T(128)}, s32[128]{0:T(128)S(1)}, bf16[5,2048,128]{1,2,0:T(8,128)(2,1)}, /*index=5*/bf16[128...) while((s32[]{:T(128)}, f32[8,128,2048]{1,2,0:T(8,128)}, s32[]{:T(128)}, s32[128]{0:T(128)S(1)}, ...), condition=%wide.region_12.12_spmd, body=%wide.region_11.11_spmd.sunk | while | flops 272629888 | bytes 18220296 | solution.py:122
  71.1 7.9 %bitcast_select_fusion.3 = f32[8,128,2048]{1,2,0:T(8,128)} fusion(f32[8,128,2048]{1,2,0:T(8,128)} %get-tuple-element.534, bf16[128,8,64]{0,2,1:T(8,128)(2,1)S(1)} %get-tuple-element.547, pred[128]{0:T(512)(128)(4,1)S(1)} %broadcast_compare_fusion.5, bf16[2048,128]{0,1:T(8,128)(2,1)S(1)} %dynamic-slice_bitcast_fusion.12), kind=kOutput, calls=%fused_computation.4.clone.1 | convolution fusion | flops 272629760 | bytes 17170944 | tf_op jit(solution)/shard_map/while/body/eval_jaxpr/while/body/rhd,md->hrm/dot_general | solution.py:115
  80.0 7.9 %bitcast_select_fusion.3 = f32[8,128,2048]{1,2,0:T(8,128)} fusion(f32[8,128,2048]{1,2,0:T(8,128)} %get-tuple-element.534, bf16[128,8,64]{0,2,1:T(8,128)(2,1)S(1)} %get-tuple-element.547, pred[128]{0:T(512)(128)(4,1)S(1)} %broadcast_compare_fusion.5, bf16[2048,128]{0,1:T(8,128)(2,1)S(1)} %dynamic-slice_bitcast_fusion.12), kind=kOutput, calls=%fused_computation.4.clone.1 | convolution fusion | flops 272629760 | bytes 17170944 | tf_op jit(solution)/shard_map/while/body/eval_jaxpr/while/body/rhd,md->hrm/dot_general | solution.py:115
  87.9 9.1 %copy.50 = f32[8,128,2048]{2,1,0:T(8,128)} copy(f32[8,128,2048]{1,2,0:T(8,128)} %get-tuple-element.506) | data formatting | bytes 16777216 | tf_op jit(solution)/shard_map/while/body/eval_jaxpr/while | solution.py:122
  97.4 4.4 select_reduce_fusion.6
  103.2 3.4 fusion.85
  108.3 19.0 %while.40 = (s32[]{:T(128)}, f32[128,8,64]{0,2,1:T(8,128)S(1)}, s32[]{:T(128)}, bf16[5,2048,128]{1,2,0:T(8,128)(2,1)}, s32[128]{0:T(128)S(1)}, /*index=5*/bf16[8...) while((s32[]{:T(128)}, f32[128,8,64]{0,2,1:T(8,128)S(1)}, s32[]{:T(128)}, ...), condition=%wide.region_16.16_spmd, body=%wide.region_15.15_spmd.sunk | while | flops 270598272 | bytes 6030599 | solution.py:165
  112.6 3.7 fusion.89
  121.8 3.7 fusion.89
  129.5 3.9 broadcast.253.clone.2
  133.4 18.0 %while.39 = (s32[]{:T(128)}, f32[8,128,2048]{1,2,0:T(8,128)}, s32[]{:T(128)}, s32[128]{0:T(128)S(1)}, bf16[5,2048,128]{1,2,0:T(8,128)(2,1)}, /*index=5*/bf16[128...) while((s32[]{:T(128)}, f32[8,128,2048]{1,2,0:T(8,128)}, s32[]{:T(128)}, s32[128]{0:T(128)S(1)}, ...), condition=%wide.region_12.12_spmd, body=%wide.region_11.11_spmd.sunk | while | flops 272629888 | bytes 18220296 | solution.py:122
  134.5 7.9 %bitcast_select_fusion.3 = f32[8,128,2048]{1,2,0:T(8,128)} fusion(f32[8,128,2048]{1,2,0:T(8,128)} %get-tuple-element.534, bf16[128,8,64]{0,2,1:T(8,128)(2,1)S(1)} %get-tuple-element.547, pred[128]{0:T(512)(128)(4,1)S(1)} %broadcast_compare_fusion.5, bf16[2048,128]{0,1:T(8,128)(2,1)S(1)} %dynamic-slice_bitcast_fusion.12), kind=kOutput, calls=%fused_computation.4.clone.1 | convolution fusion | flops 272629760 | bytes 17170944 | tf_op jit(solution)/shard_map/while/body/eval_jaxpr/while/body/rhd,md->hrm/dot_general | solution.py:115
  143.5 7.9 %bitcast_select_fusion.3 = f32[8,128,2048]{1,2,0:T(8,128)} fusion(f32[8,128,2048]{1,2,0:T(8,128)} %get-tuple-element.534, bf16[128,8,64]{0,2,1:T(8,128)(2,1)S(1)} %get-tuple-element.547, pred[128]{0:T(512)(128)(4,1)S(1)} %broadcast_compare_fusion.5, bf16[2048,128]{0,1:T(8,128)(2,1)S(1)} %dynamic-slice_bitcast_fusion.12), kind=kOutput, calls=%fused_computation.4.clone.1 | convolution fusion | flops 272629760 | bytes 17170944 | tf_op jit(solution)/shard_map/while/body/eval_jaxpr/while/body/rhd,md->hrm/dot_general | solution.py:115
  151.4 9.1 %copy.50 = f32[8,128,2048]{2,1,0:T(8,128)} copy(f32[8,128,2048]{1,2,0:T(8,128)} %get-tuple-element.506) | data formatting | bytes 16777216 | tf_op jit(solution)/shard_map/while/body/eval_jaxpr/while | solution.py:122
  160.9 4.4 select_reduce_fusion.6
  166.7 3.4 fusion.85
  171.8 19.0 %while.40 = (s32[]{:T(128)}, f32[128,8,64]{0,2,1:T(8,128)S(1)}, s32[]{:T(128)}, bf16[5,2048,128]{1,2,0:T(8,128)(2,1)}, s32[128]{0:T(128)S(1)}, /*index=5*/bf16[8...) while((s32[]{:T(128)}, f32[128,8,64]{0,2,1:T(8,128)S(1)}, s32[]{:T(128)}, ...), condition=%wide.region_16.16_spmd, body=%wide.region_15.15_spmd.sunk | while | flops 270598272 | bytes 6030599 | solution.py:165
  176.1 3.7 fusion.89
  185.3 3.7 fusion.89
  193.0 3.9 broadcast.253.clone.2
  196.9 9.0 %while.39 = (s32[]{:T(128)}, f32[8,128,2048]{1,2,0:T(8,128)}, s32[]{:T(128)}, s32[128]{0:T(128)S(1)}, bf16[5,2048,128]{1,2,0:T(8,128)(2,1)}, /*index=5*/bf16[128...) while((s32[]{:T(128)}, f32[8,128,2048]{1,2,0:T(8,128)}, s32[]{:T(128)}, s32[128]{0:T(128)S(1)}, ...), condition=%wide.region_12.12_spmd, body=%wide.region_11.11_spmd.sunk | while | flops 272629888 | bytes 18220296 | solution.py:122
  198.0 7.9 %bitcast_select_fusion.3 = f32[8,128,2048]{1,2,0:T(8,128)} fusion(f32[8,128,2048]{1,2,0:T(8,128)} %get-tuple-element.534, bf16[128,8,64]{0,2,1:T(8,128)(2,1)S(1)} %get-tuple-element.547, pred[128]{0:T(512)(128)(4,1)S(1)} %broadcast_compare_fusion.5, bf16[2048,128]{0,1:T(8,128)(2,1)S(1)} %dynamic-slice_bitcast_fusion.12), kind=kOutput, calls=%fused_computation.4.clone.1 | convolution fusion | flops 272629760 | bytes 17170944 | tf_op jit(solution)/shard_map/while/body/eval_jaxpr/while/body/rhd,md->hrm/dot_general | solution.py:115
  205.9 9.1 %copy.50 = f32[8,128,2048]{2,1,0:T(8,128)} copy(f32[8,128,2048]{1,2,0:T(8,128)} %get-tuple-element.506) | data formatting | bytes 16777216 | tf_op jit(solution)/shard_map/while/body/eval_jaxpr/while | solution.py:122
  215.4 4.4 select_reduce_fusion.6
  221.1 3.4 fusion.85
  226.2 9.8 %while.40 = (s32[]{:T(128)}, f32[128,8,64]{0,2,1:T(8,128)S(1)}, s32[]{:T(128)}, bf16[5,2048,128]{1,2,0:T(8,128)(2,1)}, s32[128]{0:T(128)S(1)}, /*index=5*/bf16[8...) while((s32[]{:T(128)}, f32[128,8,64]{0,2,1:T(8,128)S(1)}, s32[]{:T(128)}, ...), condition=%wide.region_16.16_spmd, body=%wide.region_15.15_spmd.sunk | while | flops 270598272 | bytes 6030599 | solution.py:165
  230.6 3.7 fusion.89
  238.3 3.9 broadcast.253.clone.2
  242.2 27.0 %while.39 = (s32[]{:T(128)}, f32[8,128,2048]{1,2,0:T(8,128)}, s32[]{:T(128)}, s32[128]{0:T(128)S(1)}, bf16[5,2048,128]{1,2,0:T(8,128)(2,1)}, /*index=5*/bf16[128...) while((s32[]{:T(128)}, f32[8,128,2048]{1,2,0:T(8,128)}, s32[]{:T(128)}, s32[128]{0:T(128)S(1)}, ...), condition=%wide.region_12.12_spmd, body=%wide.region_11.11_spmd.sunk | while | flops 272629888 | bytes 18220296 | solution.py:122
  243.3 7.9 %bitcast_select_fusion.3 = f32[8,128,2048]{1,2,0:T(8,128)} fusion(f32[8,128,2048]{1,2,0:T(8,128)} %get-tuple-element.534, bf16[128,8,64]{0,2,1:T(8,128)(2,1)S(1)} %get-tuple-element.547, pred[128]{0:T(512)(128)(4,1)S(1)} %broadcast_compare_fusion.5, bf16[2048,128]{0,1:T(8,128)(2,1)S(1)} %dynamic-slice_bitcast_fusion.12), kind=kOutput, calls=%fused_computation.4.clone.1 | convolution fusion | flops 272629760 | bytes 17170944 | tf_op jit(solution)/shard_map/while/body/eval_jaxpr/while/body/rhd,md->hrm/dot_general | solution.py:115
  252.3 7.9 %bitcast_select_fusion.3 = f32[8,128,2048]{1,2,0:T(8,128)} fusion(f32[8,128,2048]{1,2,0:T(8,128)} %get-tuple-element.534, bf16[128,8,64]{0,2,1:T(8,128)(2,1)S(1)} %get-tuple-element.547, pred[128]{0:T(512)(128)(4,1)S(1)} %broadcast_compare_fusion.5, bf16[2048,128]{0,1:T(8,128)(2,1)S(1)} %dynamic-slice_bitcast_fusion.12), kind=kOutput, calls=%fused_computation.4.clone.1 | convolution fusion | flops 272629760 | bytes 17170944 | tf_op jit(solution)/shard_map/while/body/eval_jaxpr/while/body/rhd,md->hrm/dot_general | solution.py:115
  261.3 7.9 %bitcast_select_fusion.3 = f32[8,128,2048]{1,2,0:T(8,128)} fusion(f32[8,128,2048]{1,2,0:T(8,128)} %get-tuple-element.534, bf16[128,8,64]{0,2,1:T(8,128)(2,1)S(1)} %get-tuple-element.547, pred[128]{0:T(512)(128)(4,1)S(1)} %broadcast_compare_fusion.5, bf16[2048,128]{0,1:T(8,128)(2,1)S(1)} %dynamic-slice_bitcast_fusion.12), kind=kOutput, calls=%fused_computation.4.clone.1 | convolution fusion | flops 272629760 | bytes 17170944 | tf_op jit(solution)/shard_map/while/body/eval_jaxpr/while/body/rhd,md->hrm/dot_general | solution.py:115
  269.2 9.1 %copy.50 = f32[8,128,2048]{2,1,0:T(8,128)} copy(f32[8,128,2048]{1,2,0:T(8,128)} %get-tuple-element.506) | data formatting | bytes 16777216 | tf_op jit(solution)/shard_map/while/body/eval_jaxpr/while | solution.py:122
  278.7 4.4 select_reduce_fusion.6
  284.4 3.4 fusion.85
  289.5 28.2 %while.40 = (s32[]{:T(128)}, f32[128,8,64]{0,2,1:T(8,128)S(1)}, s32[]{:T(128)}, bf16[5,2048,128]{1,2,0:T(8,128)(2,1)}, s32[128]{0:T(128)S(1)}, /*index=5*/bf16[8...) while((s32[]{:T(128)}, f32[128,8,64]{0,2,1:T(8,128)S(1)}, s32[]{:T(128)}, ...), condition=%wide.region_16.16_spmd, body=%wide.region_15.15_spmd.sunk | while | flops 270598272 | bytes 6030599 | solution.py:165
  293.9 3.7 fusion.89
  303.1 3.7 fusion.89
  312.2 3.7 fusion.89
  319.9 3.9 broadcast.253.clone.2
  323.8 9.0 %while.39 = (s32[]{:T(128)}, f32[8,128,2048]{1,2,0:T(8,128)}, s32[]{:T(128)}, s32[128]{0:T(128)S(1)}, bf16[5,2048,128]{1,2,0:T(8,128)(2,1)}, /*index=5*/bf16[128...) while((s32[]{:T(128)}, f32[8,128,2048]{1,2,0:T(8,128)}, s32[]{:T(128)}, s32[128]{0:T(128)S(1)}, ...), condition=%wide.region_12.12_spmd, body=%wide.region_11.11_spmd.sunk | while | flops 272629888 | bytes 18220296 | solution.py:122
  324.9 7.9 %bitcast_select_fusion.3 = f32[8,128,2048]{1,2,0:T(8,128)} fusion(f32[8,128,2048]{1,2,0:T(8,128)} %get-tuple-element.534, bf16[128,8,64]{0,2,1:T(8,128)(2,1)S(1)} %get-tuple-element.547, pred[128]{0:T(512)(128)(4,1)S(1)} %broadcast_compare_fusion.5, bf16[2048,128]{0,1:T(8,128)(2,1)S(1)} %dynamic-slice_bitcast_fusion.12), kind=kOutput, calls=%fused_computation.4.clone.1 | convolution fusion | flops 272629760 | bytes 17170944 | tf_op jit(solution)/shard_map/while/body/eval_jaxpr/while/body/rhd,md->hrm/dot_general | solution.py:115
  332.8 9.1 %copy.50 = f32[8,128,2048]{2,1,0:T(8,128)} copy(f32[8,128,2048]{1,2,0:T(8,128)} %get-tuple-element.506) | data formatting | bytes 16777216 | tf_op jit(solution)/shard_map/while/body/eval_jaxpr/while | solution.py:122
  342.3 4.4 select_reduce_fusion.6
  348.1 3.4 fusion.85
  353.2 9.8 %while.40 = (s32[]{:T(128)}, f32[128,8,64]{0,2,1:T(8,128)S(1)}, s32[]{:T(128)}, bf16[5,2048,128]{1,2,0:T(8,128)(2,1)}, s32[128]{0:T(128)S(1)}, /*index=5*/bf16[8...) while((s32[]{:T(128)}, f32[128,8,64]{0,2,1:T(8,128)S(1)}, s32[]{:T(128)}, ...), condition=%wide.region_16.16_spmd, body=%wide.region_15.15_spmd.sunk | while | flops 270598272 | bytes 6030599 | solution.py:165
  357.5 3.7 fusion.89
  365.2 3.9 broadcast.253.clone.2
  369.1 9.1 %copy.50 = f32[8,128,2048]{2,1,0:T(8,128)} copy(f32[8,128,2048]{1,2,0:T(8,128)} %get-tuple-element.506) | data formatting | bytes 16777216 | tf_op jit(solution)/shard_map/while/body/eval_jaxpr/while | solution.py:122
  378.7 4.4 select_reduce_fusion.6
  384.4 3.4 fusion.85
  390.4 6.1 %fusion.46 = f32[768,2048]{1,0:T(8,128)} fusion(bf16[768,512]{1,0:T(8,128)(2,1)S(1)} %bitcast.118, bf16[2048,2048]{1,0:T(8,128)(2,1)} %param.19, s32[]{:T(128)S(6)} %select_n.116), kind=kOutput, calls=%fused_computation.63 | convolution fusion | flops 1610612736 | bytes 9175044 | tf_op jit(solution)/shard_map/dot_general | solution.py:183
  396.4 129.0 %reduce-scatter.2.cloned.1.call-done = f32[768,512]{1,0:T(8,128)} async-done(((f32[768,2048]{1,0:T(8,128)}), f32[768,512]{1,0:T(8,128)}) %reduce-scatter.2.cloned.1.call-update) | async-done | bytes 1572880 | tf_op jit(solution)/shard_map/reduce_scatter | solution.py:184
  525.4 2.4 convert_element_type.36
  (182 shorter events, 60.2 us)
Async XLA Ops:
  6.5 12.8 %copy-start = (bf16[2048,512]{1,0:T(8,128)(2,1)S(1)}, bf16[2048,512]{1,0:T(8,128)(2,1)}, u32[]{:S(2)}) copy-start(bf16[2048,512]{1,0:T(8,128)(2,1)} %param.17) | copy-start | bytes 6291460
  6.5 8.7 %copy-start.5 = (s32[40]{0:T(128)S(1)}, s32[40]{0:T(128)}, u32[]{:S(2)}) copy-start(s32[40]{0:T(128)} %param.23) | copy-start | bytes 484
  6.5 9.1 %copy-start.6 = (s32[40]{0:T(128)S(1)}, s32[40]{0:T(128)}, u32[]{:S(2)}) copy-start(s32[40]{0:T(128)} %param.22) | copy-start | bytes 484
  6.5 48.2 %all-gather.3.cloned.1.call-start = ((), (), s32[]{:S(2)}) async-start(), calls=%async_computation.2 | async-start | bytes 4718592 | tf_op jit(solution)/shard_map/all_gather | solution.py:94
  12.1 7.2 %copy-start.7 = (f32[2048]{0:T(1024)S(1)}, f32[2048]{0:T(1024)}, u32[]{:S(2)}) copy-start(f32[2048]{0:T(1024)} %param.16) | copy-start | bytes 24580
  15.1 510.3 %reduce-scatter.2.cloned.1.call-start = ((), (), s32[]{:S(2)}) async-start(), calls=%async_computation.1 | async-start | bytes 7864320 | tf_op jit(solution)/shard_map/reduce_scatter | solution.py:184
  15.9 3.4 copy-start.3
  59.5 4.6 copy-start.4
  97.4 5.8 %copy-start.2 = (f32[8,128,2048]{2,1,0:T(8,128)S(1)}, f32[8,128,2048]{2,1,0:T(8,128)}, u32[]{:S(2)}) copy-start(f32[8,128,2048]{2,1,0:T(8,128)} %copy.50) | copy-start | bytes 25165828 | tf_op jit(solution)/shard_map/while
  160.9 5.8 %copy-start.2 = (f32[8,128,2048]{2,1,0:T(8,128)S(1)}, f32[8,128,2048]{2,1,0:T(8,128)}, u32[]{:S(2)}) copy-start(f32[8,128,2048]{2,1,0:T(8,128)} %copy.50) | copy-start | bytes 25165828 | tf_op jit(solution)/shard_map/while
  215.4 5.8 %copy-start.2 = (f32[8,128,2048]{2,1,0:T(8,128)S(1)}, f32[8,128,2048]{2,1,0:T(8,128)}, u32[]{:S(2)}) copy-start(f32[8,128,2048]{2,1,0:T(8,128)} %copy.50) | copy-start | bytes 25165828 | tf_op jit(solution)/shard_map/while
  278.7 5.8 %copy-start.2 = (f32[8,128,2048]{2,1,0:T(8,128)S(1)}, f32[8,128,2048]{2,1,0:T(8,128)}, u32[]{:S(2)}) copy-start(f32[8,128,2048]{2,1,0:T(8,128)} %copy.50) | copy-start | bytes 25165828 | tf_op jit(solution)/shard_map/while
  342.3 5.8 %copy-start.2 = (f32[8,128,2048]{2,1,0:T(8,128)S(1)}, f32[8,128,2048]{2,1,0:T(8,128)}, u32[]{:S(2)}) copy-start(f32[8,128,2048]{2,1,0:T(8,128)} %copy.50) | copy-start | bytes 25165828 | tf_op jit(solution)/shard_map/while
  378.6 5.8 %copy-start.2 = (f32[8,128,2048]{2,1,0:T(8,128)S(1)}, f32[8,128,2048]{2,1,0:T(8,128)}, u32[]{:S(2)}) copy-start(f32[8,128,2048]{2,1,0:T(8,128)} %copy.50) | copy-start | bytes 25165828 | tf_op jit(solution)/shard_map/while
  396.4 131.4 %copy-start.1 = (bf16[2048,512]{1,0:T(8,128)(2,1)S(1)}, bf16[2048,512]{1,0:T(8,128)(2,1)}, u32[]{:S(2)}) copy-start(bf16[2048,512]{1,0:T(8,128)(2,1)} %param.17) | copy-start | bytes 6291460
Sparse Core Ops, SparseCore 0:
  15.3 39.4 all-gather.2
  396.6 128.8 reduce-scatter.1
where the time goes:
time: 538 us; the launch traced here: 535 us
  waiting for transfers between devices  154 us (29%)
  matrix products  124 us (23%)
  local copies, waits for them, and re-layouts  121 us (22%)
  other arithmetic  74.7 us (14%)
  loops' own time  46.4 us (9%)
  between operations  13.6 us (3%)
    reduce_scatter x1, waiting for transfers between devices, body(): lax.psum_scatter(partial_terms, 'tensor', scatter_dimension=1, tiled=True)  129 us
    dot_general x9, matrix products, add_scores(): jnp.einsum('rhd,md->hrm', block_query, keys_here, preferred_element_type=...  71 us
    while x6, local copies, waits for them, and re-layouts, one_block(): lax.fori_loop(first_request, last_request + 1, add_scores, jnp.zeros((res...  54.6 us
    another operation x6, loops' own time, one_block(): lax.fori_loop(first_request, last_request + 1, add_values, weighted)  37.9 us
    dot_general x9, matrix products, add_values(): jnp.einsum('hrm,md->rhd', chosen, values_here, preferred_element_type=jnp...  33 us
    reduce_max x6, other arithmetic, one_block(): jnp.max(jnp.where(prefix_mask[None], prefix_scores, MASKED_SCORE), axis=2)  26.5 us
    reduce_sum x12, other arithmetic, one_block(): row_total = jnp.sum(prefix_raw, axis=2) + jnp.sum(suffix_raw, axis=2)  25.4 us
    all_gather x1, waiting for transfers between devices, body(): gathered = lax.all_gather(outgoing, 'seq', axis=0, tiled=True)  25.1 us
  transfers between devices with their start and end apart: 2, of which 2 were waited for; matrix products, arithmetic and copies ran while one was open for 3% of the time, Pallas kernels for 0%

commit v1 on v0

v1 whole, which is shorter than its diff:
```python
import functools
import math

import jax
import jax.numpy as jnp
from jax import lax
from jax.experimental import pallas as pl
from jax.experimental.pallas import tpu as pltpu
from jax.sharding import PartitionSpec as P

QUERY_HEADS = 32
KEY_VALUE_HEADS = 4
HEAD_SIZE = 64
WINDOW_LENGTH = 2048
DEVICE_REQUESTS = 5
PPG = 64
WP = 16
PAGE = 128
VROWS = 80
MASKED_SCORE = -1e30
SCALE = HEAD_SIZE ** (-0.5) * math.log2(math.e)


def normalize(tokens, norm_gain):
    widened = tokens.astype(jnp.float32)
    factor = lax.rsqrt(jnp.mean(widened * widened, axis=-1, keepdims=True) + 1e-05)
    return (widened * factor * norm_gain).astype(jnp.bfloat16)


def lookup_rows(table, wanted):
    matches = wanted[:, None] == lax.iota(jnp.int32, table.shape[0])[None, :]
    return jnp.sum(jnp.where(matches[:, :, None], table[None, :, :], 0), axis=1)


def pack_kernel(count, slot_ref, cache_ref, out_ref, sems):
    for i in range(count):
        pltpu.make_async_copy(
            cache_ref.at[slot_ref[i], slot_ref[count]], out_ref.at[i], sems.at[i]
        ).start()
    for i in range(count):
        pltpu.make_async_copy(cache_ref.at[0, 0], out_ref.at[i], sems.at[i]).wait()


def attention_kernel(
    rows_per_block, bounds_ref, page_ref, pages_ref, fresh_ref, q_ref, out_ref, kv, vt
):
    block_count, _, width = q_ref.shape
    fresh_count = fresh_ref.shape[0]
    prefix_pages = DEVICE_REQUESTS * WP
    vt[:, HEAD_SIZE:, :] = jnp.ones((vt.shape[0], VROWS - HEAD_SIZE, PAGE), jnp.bfloat16)
    out_ref[...] = jnp.zeros_like(out_ref)

    def place(slot, page):
        kv[slot] = page
        vt[slot, :HEAD_SIZE, :] = jnp.transpose(page)[HEAD_SIZE:]

    def fill(i, carry):
        place(i, pages_ref[page_ref[i]])
        return carry

    lax.fori_loop(0, prefix_pages, fill, 0, unroll=4)
    for i in range(fresh_count):
        place(prefix_pages + i, fresh_ref[i])

    key_index = lax.broadcasted_iota(jnp.int32, (PAGE, width), 0)
    lane_row = lax.broadcasted_iota(jnp.int32, (1, width), 1) % rows_per_block

    def group(slots, masks, query, top, total):
        scores = []
        for slot, mask in zip(slots, masks):
            one = jnp.dot(kv[slot], query, preferred_element_type=jnp.float32) * SCALE
            scores.append(one if mask is None else jnp.where(mask, one, MASKED_SCORE))
        peak = functools.reduce(jnp.maximum, scores)
        peak = jnp.max(peak, axis=0, keepdims=True)
        new_top = peak if top is None else jnp.maximum(top, peak)
        weights = jnp.concatenate(
            [jnp.exp2(one - new_top).astype(jnp.bfloat16) for one in scores], axis=0
        )
        values = jnp.concatenate([vt[slot] for slot in slots], axis=1)
        added = jnp.dot(values, weights, preferred_element_type=jnp.float32)
        if total is not None:
            added = added + total * jnp.exp2(top - new_top)
        return new_top, added

    def one_item(request, block):
        first_row = block * rows_per_block
        start = bounds_ref[request]
        end = bounds_ref[DEVICE_REQUESTS + request]
        query = q_ref[block]
        row = lane_row + first_row
        position = row - start
        first_fresh = start // PAGE
        last_fresh = first_row // PAGE
        first_page = (jnp.maximum(first_row - start, 0) + 1) // PAGE
        base = request * WP
        inside = 14 - first_page
        several = last_fresh > first_fresh

        def plain(u):
            wanted = prefix_pages + first_fresh + 1 + (u - inside)
            return jnp.where(u < inside, base + first_page + 2 + u, wanted)

        count = inside + jnp.maximum(last_fresh - first_fresh - 1, 0)
        slots = [
            base + first_page,
            base + first_page + 1,
            prefix_pages + first_fresh,
            prefix_pages + last_fresh,
            plain(12),
            jnp.where(count > 13, plain(13), base),
        ]
        fresh_low = start - first_fresh * PAGE
        last_high = jnp.where(several, row - last_fresh * PAGE, -1)
        masks = [
            key_index > position - first_page * PAGE,
            key_index > position - (first_page + 1) * PAGE,
            (key_index <= row - first_fresh * PAGE) & (key_index >= fresh_low),
            key_index <= last_high,
            None,
            key_index < jnp.where(count > 13, PAGE, 0),
        ]
        top, total = group(slots, masks, query, None, None)
        for part in range(2):
            slots = [plain(part * 6 + u) for u in range(6)]
            top, total = group(slots, [None] * 6, query, top, total)
        result = total[:HEAD_SIZE] / total[HEAD_SIZE : HEAD_SIZE + 1]
        mine = (row >= start) & (row < end)
        out_ref[block] = jnp.where(
            mine, result, out_ref[block].astype(jnp.float32)
        ).astype(jnp.bfloat16)
        return block

    def one_block(block, carry):
        first_row = block * rows_per_block
        first = 0
        last = -1
        for r in range(DEVICE_REQUESTS):
            first = first + (bounds_ref[DEVICE_REQUESTS + r] <= first_row).astype(jnp.int32)
            last = last + (bounds_ref[r] < first_row + rows_per_block).astype(jnp.int32)
        lax.fori_loop(first, last + 1, one_item, block)
        return carry

    lax.fori_loop(0, block_count, one_block, 0)


def body(
    tokens,
    norm_gain,
    query_weight,
    key_value_matrix,
    out_weight,
    cache_pages,
    page_table,
    request_lengths,
    request_groups,
):
    seq_count = lax.axis_size("seq")
    seq_index = lax.axis_index("seq")
    tensor_index = lax.axis_index("tensor")
    tensor_count = lax.axis_size("tensor")
    row_count = tokens.shape[0]
    heads = query_weight.shape[1] // HEAD_SIZE
    key_value_head = tensor_index * heads // (QUERY_HEADS // KEY_VALUE_HEADS)
    group_count = page_table.shape[0]
    per_owner = WP // seq_count
    pages_here = cache_pages.shape[0]
    send_count = group_count * per_owner

    tail_ids = page_table[:, PPG - WP :]
    holder = tail_ids // pages_here
    local_slot = tail_ids % pages_here
    earlier = lax.iota(jnp.int32, WP)[:, None] > lax.iota(jnp.int32, WP)[None, :]
    same_owner = holder[:, :, None] == holder[:, None, :]
    tail_rank = jnp.sum((same_owner & earlier[None, :, :]).astype(jnp.int32), axis=2)
    tail_hit = (holder == seq_index)[:, :, None] & (
        tail_rank[:, :, None] == lax.iota(jnp.int32, per_owner)[None, None, :]
    )
    tail_pick = jnp.sum(jnp.where(tail_hit, local_slot[:, :, None], 0), axis=1).reshape(-1)
    packed = pl.pallas_call(
        functools.partial(pack_kernel, send_count),
        out_shape=jax.ShapeDtypeStruct((send_count, PAGE, 2 * HEAD_SIZE), jnp.bfloat16),
        in_specs=[
            pl.BlockSpec(memory_space=pltpu.SMEM),
            pl.BlockSpec(memory_space=pl.ANY),
        ],
        out_specs=pl.BlockSpec(memory_space=pl.ANY),
        scratch_shapes=[pltpu.SemaphoreType.DMA((send_count,))],
        name="pack_pages",
    )(jnp.concatenate([tail_pick, key_value_head[None].astype(jnp.int32)]), cache_pages)
    gathered = lax.all_gather(packed, "seq", axis=0, tiled=True)

    normed = normalize(tokens, norm_gain)
    query_rows = jnp.dot(normed, query_weight, preferred_element_type=jnp.float32).astype(
        jnp.bfloat16
    )
    head_weight = lax.dynamic_index_in_dim(key_value_matrix, key_value_head, 1, keepdims=False)
    fresh = jnp.dot(normed, head_weight, preferred_element_type=jnp.float32).astype(jnp.bfloat16)
    fresh = fresh.reshape(row_count // PAGE, PAGE, 2 * HEAD_SIZE)
    rows_per_block = min(PAGE, 256 // heads)
    block_count = row_count // rows_per_block
    width = heads * rows_per_block
    query = query_rows.reshape(block_count, rows_per_block, heads, HEAD_SIZE)
    query = jnp.transpose(query, (0, 3, 2, 1)).reshape(block_count, HEAD_SIZE, width)
    query = jnp.concatenate([query, jnp.zeros_like(query)], axis=1)

    lengths = lax.dynamic_slice_in_dim(
        request_lengths, seq_index * DEVICE_REQUESTS, DEVICE_REQUESTS
    )
    groups = lax.dynamic_slice_in_dim(
        request_groups, seq_index * DEVICE_REQUESTS, DEVICE_REQUESTS
    )
    ends = jnp.cumsum(lengths)
    bounds = jnp.concatenate([ends - lengths, ends])
    where_from = (
        lookup_rows(holder, groups) * send_count
        + groups[:, None] * per_owner
        + lookup_rows(tail_rank, groups)
    ).reshape(-1)
    slots = DEVICE_REQUESTS * WP + row_count // PAGE
    attended = pl.pallas_call(
        functools.partial(attention_kernel, rows_per_block),
        out_shape=jax.ShapeDtypeStruct((block_count, HEAD_SIZE, width), jnp.bfloat16),
        in_specs=[pl.BlockSpec(memory_space=pltpu.SMEM)] * 2
        + [pl.BlockSpec(memory_space=pltpu.VMEM)] * 3,
        out_specs=pl.BlockSpec(memory_space=pltpu.VMEM),
        scratch_shapes=[
            pltpu.VMEM((slots, PAGE, 2 * HEAD_SIZE), jnp.bfloat16),
            pltpu.VMEM((slots, VROWS, PAGE), jnp.bfloat16),
        ],
        compiler_params=pltpu.CompilerParams(vmem_limit_bytes=40 * 1024 * 1024),
        name="attend",
    )(bounds, where_from, gathered, fresh, query)
    attended = attended.reshape(block_count, HEAD_SIZE, heads, rows_per_block)
    attended = jnp.transpose(attended, (0, 3, 2, 1)).reshape(row_count, heads * HEAD_SIZE)
    everything = lax.all_gather(attended, "tensor", axis=1, tiled=True)
    columns = out_weight.shape[1] // tensor_count
    my_columns = lax.dynamic_slice_in_dim(out_weight, tensor_index * columns, columns, 1)
    return jnp.dot(everything, my_columns, preferred_element_type=jnp.float32).astype(jnp.bfloat16)


def solution(mesh):
    return jax.shard_map(
        body,
        mesh=mesh,
        in_specs=(
            P("seq", None),
            P(),
            P(None, "tensor"),
            P(),
            P(),
            P("seq", None, None, None),
            P(),
            P(),
            P(),
        ),
        out_specs=P("seq", "tensor"),
        check_vma=False,
    )
```

time: 538 us -> 195 us (0.36)
  matrix products: 124 us -> 8.09 us
  local copies, waits for them, and re-layouts: 121 us -> 22.4 us
  other arithmetic: 74.7 us -> 6.18 us
  waiting for transfers between devices: 154 us -> 101 us
  loops' own time: 46.4 us -> 0 us
  Pallas kernels: 0 us -> 43.5 us
    reduce_scatter x1 -> x0, waiting for transfers between devices: 129 us -> none  [body(): lax.psum_scatter(partial_terms, 'tensor', scatter_dimension=1, tiled=True)]
    dot_general x31 -> x1, matrix products: 119 us -> 5.21 us  [body(): jnp.dot(everything, my_columns, preferred_element_type=jnp.float32)]
    all_gather x1 -> x2, waiting for transfers between devices: 25.1 us -> 101 us  [the longest x1 78.1 us: body(): everything = lax.all_gather(attended, 'tensor', axis=1, tiled=True)]
    while x18 -> x0, local copies, waits for them, and re-layouts: 56.7 us -> none  [the longest x6 54.6 us: one_block(): lax.fori_loop(first_request, last_request + 1, add_scores, jnp.zeros((res...]
    another operation x13 -> x0, loops' own time: 46.4 us -> none  [the longest x6 37.9 us: one_block(): lax.fori_loop(first_request, last_request + 1, add_values, weighted)]
    pallas_call x0 -> x2, Pallas kernels: none -> 43.5 us  [the longest x1 25.6 us: body(): pl.pallas_call(functools.partial(attention_kernel, rows_per_block), out_s...]
    reduce_max x12 -> x0, other arithmetic: 30.8 us -> none  [the longest x6 26.5 us: one_block(): jnp.max(jnp.where(prefix_mask[None], prefix_scores, MASKED_SCORE), axis=2)]
    reduce_sum x15 -> x1, other arithmetic: 25.8 us -> 0.15 us  [body(): jnp.sum(jnp.where(tail_hit, local_slot[:, :, None], 0), axis=1).reshape(-1)]
  transfers between devices with their start and end apart: 2 -> 2, of which waited for: 2 -> 2; matrix products, arithmetic and copies ran while one was open for 3% -> 8% of each run, Pallas kernels for 0% -> 0%
where the time goes in v1:
time: 195 us
  waiting for transfers between devices  101 us (52%)
  Pallas kernels  43.5 us (22%)
  local copies, waits for them, and re-layouts  22.4 us (11%)
  between operations  13.5 us (7%)
  matrix products  8.09 us (4%)
  other arithmetic  6.18 us (3%)
    all_gather x1, waiting for transfers between devices, body(): everything = lax.all_gather(attended, 'tensor', axis=1, tiled=True)  78.1 us
    pallas_call x1, Pallas kernels, body(): pl.pallas_call(functools.partial(attention_kernel, rows_per_block), out_s...  25.6 us
    all_gather x1, waiting for transfers between devices, body(): gathered = lax.all_gather(packed, 'seq', axis=0, tiled=True)  22.8 us
    pallas_call x1, Pallas kernels, body(): pl.pallas_call(functools.partial(pack_kernel, send_count), out_shape=jax....  17.9 us
    dot_general x1, matrix products, body(): jnp.dot(everything, my_columns, preferred_element_type=jnp.float32)  5.21 us
    reshape x2, local copies, waits for them, and re-layouts, body(): query = query_rows.reshape(block_count, rows_per_block, heads, HEAD_SIZE)  4.68 us
  transfers between devices with their start and end apart: 2, of which 2 were waited for; matrix products, arithmetic and copies ran while one was open for 8% of the time, Pallas kernels for 0%

profile of v1, /device:TPU:0, one launch (start us, length us, event | category | flops | bytes accessed | tf_op | source)
XLA Modules:
  0.0 194.8 jit_solution(15059677424561467988)
XLA Ops:
  6.5 0.0 copy-start
  6.5 0.0 all-gather.3.cloned.1.call-start
  6.6 0.9 broadcast_compare_fusion
  7.5 0.8 add_select_fusion
  8.2 0.3 convert_reduce_fusion
  8.5 0.2 select_reduce_fusion.2
  8.7 0.1 copy.21
  8.8 0.1 reshape.105
  8.8 0.7 pad_add_fusion.1.slot_ref
  9.5 0.0 copy-start.6
  9.5 0.0 copy-start.5
  9.5 17.9 %pack_pages.1 = bf16[16,128,128]{2,1,0:T(8,128)(2,1)} custom-call(s32[17]{0:T(128)} %pad_add_fusion.1.slot_ref, bf16[64,4,128,128]{3,2,1,0:T(8,128)(2,1)} %cache_ref.1), custom_call_target="tpu_custom_call" | custom-call | tf_op jit(solution)/shard_map/pack_pages/pallas_call | solution.py:179
  27.5 0.0 copy-start.7
  27.5 0.0 all-gather.3.cloned.1.call-update
  27.5 0.0 all-gather.5.cloned.1.call-start
  27.6 0.0 copy-done.6
  27.6 0.1 dynamic-slice_bitcast_fusion
  27.6 0.2 reduce-window.9
  27.8 0.0 copy-done.5
  27.8 0.1 broadcast_multiply_fusion
  27.9 0.1 iota_compare_fusion.2
  28.0 0.1 select_reduce_fusion.1
  28.1 0.1 add_add_fusion
  28.1 0.1 add.53.page_ref
  28.2 0.0 copy-start.3
  28.2 2.7 %fusion = f32[768]{0:T(1024)S(1)} fusion(bf16[768,2048]{1,0:T(8,128)(2,1)} %param.9), kind=kLoop, calls=%fused_computation.2 | loop fusion | flops 4717824 | bytes 3148800 | tf_op jit(solution)/shard_map/reduce_sum | solution.py:26
  31.0 0.0 copy-done
  31.0 0.0 copy-done.7
  31.0 0.1 copy-done.3
  31.1 1.8 convolution_convert_fusion
  32.9 1.7 reshape.107
  34.6 2.9 %copy.23 = bf16[24,32,8,64]{3,1,2,0:T(8,128)(2,1)} copy(bf16[24,32,8,64]{3,2,1,0:T(8,128)(2,1)} %reshape.107) | data formatting | bytes 1572864 | tf_op jit(solution)/shard_map/reshape | solution.py:202
  37.6 1.7 copy.24
  39.3 0.0 copy-start.4
  39.3 1.4 concatenate.11.q_ref
  40.7 0.1 dynamic-slice_subtract_fusion
  40.8 0.1 pad_add_fusion.bounds_ref
  40.8 2.3 %constant_dynamic-slice_fusion = bf16[2048,1,128]{2,1,0:T(2,128)(2,1)S(1)} fusion(bf16[2048,4,128]{2,1,0:T(4,128)(2,1)} %param.12, s32[]{:T(128)S(6)} %select_n.45), kind=kLoop, calls=%fused_computation.34 | loop fusion | bytes 1048580 | tf_op jit(solution)/shard_map/jit(dynamic_index_in_dim)/dynamic_slice | solution.py:196
  43.2 0.0 copy-done.4
  43.2 1.0 convolution_convert_fusion.1
  44.2 22.8 %all-gather.3.cloned.1.call-done.pages_ref = bf16[128,128,128]{2,1,0:T(8,128)(2,1)} async-done(((bf16[16,128,128]{2,1,0:T(8,128)(2,1)}), bf16[128,128,128]{2,1,0:T(8,128)(2,1)}) %all-gather.3.cloned.1.call-update) | async-done | bytes 4194320 | tf_op jit(solution)/shard_map/all_gather | solution.py:190
  67.1 0.0 copy-start.1
  67.1 1.4 copy-done.1
  68.5 0.0 copy-start.2
  68.5 2.2 %copy-done.2 = bf16[128,128,128]{2,1,0:T(8,128)(2,1)S(1)} copy-done((bf16[128,128,128]{2,1,0:T(8,128)(2,1)S(1)}, bf16[128,128,128]{2,1,0:T(8,128)(2,1)}, u32[]{:S(2)}) %copy-start.2) | copy-done | bytes 4194328
  70.7 25.6 %attend.1 = bf16[24,64,256]{2,1,0:T(8,128)(2,1)S(1)} custom-call(s32[10]{0:T(128)S(1)} %pad_add_fusion.bounds_ref, s32[80]{0:T(128)S(1)} %add.53.page_ref, bf16[128,128,128]{2,1,0:T(8,128)(2,1)S(1)} %copy-done.2, bf16[6,128,128]{2,1,0:T(8,128)(2,1)S(1)} %bitcast.19, bf16[24,128,256]{2,1,0:T(8,128)(2,1)S(1)} %copy-done.1), custom_call_target="tpu_custom_call" | custom-call | tf_op jit(solution)/shard_map/attend/pallas_call | solution.py:220
  96.3 1.6 copy.25
  97.8 3.3 %copy.26 = bf16[24,32,8,64]{3,2,1,0:T(8,128)(2,1)} copy(bf16[24,32,8,64]{3,1,2,0:T(8,128)(2,1)} %bitcast.21) | data formatting | bytes 1572864 | tf_op jit(solution)/shard_map/transpose | solution.py:234
  101.1 3.5 %reshape.110 = bf16[768,512]{1,0:T(8,128)(2,1)} reshape(bf16[24,32,8,64]{3,2,1,0:T(8,128)(2,1)} %copy.26) | data formatting | bytes 1572864 | tf_op jit(solution)/shard_map/reshape | solution.py:234
  104.6 0.0 all-gather.5.cloned.1.call-update
  104.6 78.1 %all-gather.5.cloned.1.call-done = bf16[768,2048]{1,0:T(8,128)(2,1)} async-done(((bf16[768,512]{1,0:T(8,128)(2,1)}), bf16[768,2048]{1,0:T(8,128)(2,1)}) %all-gather.5.cloned.1.call-update) | async-done | bytes 3145744 | tf_op jit(solution)/shard_map/all_gather | solution.py:235
  182.7 5.2 %fusion.5 = bf16[768,512]{1,0:T(8,128)(2,1)} fusion(bf16[768,2048]{1,0:T(8,128)(2,1)} %all-gather.5.cloned.1.call-done, bf16[2048,2048]{1,0:T(8,128)(2,1)} %param.13, s32[]{:T(128)S(6)} %select_n.46), kind=kOutput, calls=%fused_computation.8 | convolution fusion | flops 1611005952 | bytes 6029316 | tf_op jit(solution)/shard_map/dot_general | solution.py:238
  (2 shorter events, 0.0 us)
Async XLA Ops:
  6.5 24.4 %copy-start = (bf16[2048,512]{1,0:T(8,128)(2,1)S(1)}, bf16[2048,512]{1,0:T(8,128)(2,1)}, u32[]{:S(2)}) copy-start(bf16[2048,512]{1,0:T(8,128)(2,1)} %param.11) | copy-start | bytes 6291460
  6.5 60.5 %all-gather.3.cloned.1.call-start = ((), (), s32[]{:S(2)}) async-start(), calls=%async_computation | async-start | bytes 4718592 | tf_op jit(solution)/shard_map/all_gather | solution.py:190
  9.5 18.0 %copy-start.6 = (s32[40]{0:T(128)S(1)}, s32[40]{0:T(128)}, u32[]{:S(2)}) copy-start(s32[40]{0:T(128)} %param.16) | copy-start | bytes 484
  9.5 18.3 %copy-start.5 = (s32[40]{0:T(128)S(1)}, s32[40]{0:T(128)}, u32[]{:S(2)}) copy-start(s32[40]{0:T(128)} %param.17) | copy-start | bytes 484
  27.5 3.5 %copy-start.7 = (f32[2048]{0:T(1024)S(1)}, f32[2048]{0:T(1024)}, u32[]{:S(2)}) copy-start(f32[2048]{0:T(1024)} %param.10) | copy-start | bytes 24580
  27.5 155.2 %all-gather.5.cloned.1.call-start = ((), (), s32[]{:S(2)}) async-start(), calls=%async_computation.1 | async-start | bytes 3932160 | tf_op jit(solution)/shard_map/all_gather | solution.py:235
  28.2 2.8 %copy-start.3 = (bf16[768,2048]{1,0:T(8,128)(2,1)S(1)}, bf16[768,2048]{1,0:T(8,128)(2,1)}, u32[]{:S(2)}) copy-start(bf16[768,2048]{1,0:T(8,128)(2,1)} %param.9) | copy-start | bytes 9437188
  39.3 3.9 %copy-start.4 = (bf16[768,2048]{1,0:T(8,128)(2,1)S(1)}, bf16[768,2048]{1,0:T(8,128)(2,1)}, u32[]{:S(2)}) copy-start(bf16[768,2048]{1,0:T(8,128)(2,1)} %param.9) | copy-start | bytes 9437188
  67.1 1.4 copy-start.1
  68.5 2.2 %copy-start.2 = (bf16[128,128,128]{2,1,0:T(8,128)(2,1)S(1)}, bf16[128,128,128]{2,1,0:T(8,128)(2,1)}, u32[]{:S(2)}) copy-start(bf16[128,128,128]{2,1,0:T(8,128)(2,1)} %all-gather.3.cloned.1.call-done.pages_ref) | copy-start | bytes 12582916
Sparse Core Ops, SparseCore 0:
  27.6 39.4 all-gather.2
  104.7 77.9 all-gather.4
